TPU v7x, 256 devices: a whole 4x4x8 slice. The times are simulated.
256 devices in a mesh: dp: 32 (over z, x), replica: 8 (over y, core).
Axes of the slice: x: 4, y: 4, z: 8, core: 2. Of those that a mesh axis runs over, the one named last changes fastest.
Arguments:
- activations: bfloat16 [114688, 8192], P(('dp', 'replica')), may hold values from -24 to 24
- out_grads: bfloat16 [114688, 256], P(('dp', 'replica')), may hold values from -0.046875 to 0.046875
- master: float32 [8192, 256], P(('dp', 'replica')), may hold values from -6 to 6
- first_moment: float32 [8192, 256], P(('dp', 'replica')), may hold values from -6 to 6
- second_moment: float32 [8192, 256], P(('dp', 'replica')), may hold values from 0.5 to 2
Outputs:
- grad_total: float32 [8192, 256], P(('dp', 'replica'))
- new_master: float32 [8192, 256], P(('dp', 'replica'))
- new_first: float32 [8192, 256], P(('dp', 'replica'))
- new_second: float32 [8192, 256], P(('dp', 'replica'))
- weights: bfloat16 [8192, 256], replicated
All inputs are finite; a program needn't handle non-finite values.
Results may differ from a plain program's by a relative error of at most 0.0095.
Values may be sent and summed in bfloat16 or wider, within the bound.
A program may use at most 64 MiB of HBM per device.

v0:
```python
import jax
import jax.numpy as jnp
from jax import lax
from jax.sharding import PartitionSpec as P

beta_first = 0.9
beta_second = 0.999
learn_rate = 0.2
decay_rate = 0.1
adam_eps = 1e-08
step_count = 100


def body(activations, out_grads, master, first_moment, second_moment):
    term = jnp.einsum("tr,tc->rc", activations, out_grads, preferred_element_type=jnp.float32)
    code = lax.optimization_barrier(term.astype(jnp.bfloat16))
    grad_total = lax.psum_scatter(
        code.astype(jnp.float32), ("dp", "replica"), scatter_dimension=0, tiled=True
    )
    new_first = beta_first * first_moment + (1.0 - beta_first) * grad_total
    new_second = beta_second * second_moment + (1.0 - beta_second) * grad_total * grad_total
    first_hat = new_first / (1.0 - beta_first**step_count)
    second_hat = new_second / (1.0 - beta_second**step_count)
    new_master = master - learn_rate * (
        first_hat / (jnp.sqrt(second_hat) + adam_eps) + decay_rate * master
    )
    rounded = new_master.astype(jnp.bfloat16)
    weights = lax.all_gather(rounded, ("dp", "replica"), axis=0, tiled=True)
    return (grad_total, new_master, new_first, new_second, weights)


def solution(mesh):
    in_specs = (
        P(("dp", "replica"), None),
        P(("dp", "replica"), None),
        P(("dp", "replica"), None),
        P(("dp", "replica"), None),
        P(("dp", "replica"), None),
    )
    out_specs = (
        P(("dp", "replica"), None),
        P(("dp", "replica"), None),
        P(("dp", "replica"), None),
        P(("dp", "replica"), None),
        P(),
    )
    return jax.shard_map(body, mesh=mesh, in_specs=in_specs, out_specs=out_specs, check_vma=False)
```

profile of v0, /device:TPU:1, one launch (start us, length us, event | category | flops | bytes accessed | tf_op | source)
XLA Modules:
  0.0 1431.1 jit_solution(2816040165554024998)
XLA Ops:
  7.2 0.0 copy-start
  7.2 0.0 reduce-scatter.2.cloned.1.call-start
  7.2 0.9 copy-done
  8.1 5.5 convolution_convert_fusion
  13.7 3.9 convert_element_type.10
  17.6 0.0 copy-start.1
  17.6 0.0 copy-start.2
  17.6 0.0 copy-start.3
  17.6 0.0 reduce-scatter.2.cloned.1.call-update
  17.6 0.0 all-gather.2.cloned.1.call-start
  17.6 1277.4 %reduce-scatter.2.cloned.1.call-done = f32[32,256]{1,0:T(8,128)} async-done(((f32[8192,256]{1,0:T(8,128)}), f32[32,256]{1,0:T(8,128)}) %reduce-scatter.2.cloned.1.call-update) | async-done | bytes 32784 | tf_op jit(solution)/shard_map/reduce_scatter | solution.py:17
  1295.1 0.0 copy-done.1
  1295.1 0.0 copy-done.2
  1295.1 0.0 copy-done.3
  1295.1 1.4 fusion.1
  1296.5 0.0 all-gather.2.cloned.1.call-update
  1296.5 123.3 %all-gather.2.cloned.1.call-done = bf16[8192,256]{1,0:T(8,128)(2,1)} async-done(((bf16[32,256]{1,0:T(8,128)(2,1)}), bf16[8192,256]{1,0:T(8,128)(2,1)}) %all-gather.2.cloned.1.call-update) | async-done | bytes 4194320 | tf_op jit(solution)/shard_map/all_gather | solution.py:28
  1419.8 4.5 copy.11
Async XLA Ops:
  7.2 0.9 copy-start
  7.2 1287.9 %reduce-scatter.2.cloned.1.call-start = ((), (), s32[]{:S(2)}) async-start(), calls=%async_computation.1 | async-start | bytes 8421376 | tf_op jit(solution)/shard_map/reduce_scatter | solution.py:17
  17.6 1277.5 %copy-start.1 = (f32[32,256]{1,0:T(8,128)S(1)}, f32[32,256]{1,0:T(8,128)}, u32[]{:S(2)}) copy-start(f32[32,256]{1,0:T(8,128)} %param.7) | copy-start | bytes 98308
  17.6 1277.5 %copy-start.2 = (f32[32,256]{1,0:T(8,128)S(1)}, f32[32,256]{1,0:T(8,128)}, u32[]{:S(2)}) copy-start(f32[32,256]{1,0:T(8,128)} %param.8) | copy-start | bytes 98308
  17.6 1277.5 %copy-start.3 = (f32[32,256]{1,0:T(8,128)S(1)}, f32[32,256]{1,0:T(8,128)}, u32[]{:S(2)}) copy-start(f32[32,256]{1,0:T(8,128)} %param.9) | copy-start | bytes 98308
  17.6 1402.2 %all-gather.2.cloned.1.call-start = ((), (), s32[]{:S(2)}) async-start(), calls=%async_computation.2 | async-start | bytes 4210688 | tf_op jit(solution)/shard_map/all_gather | solution.py:28
Sparse Core Ops, SparseCore 0:
  17.7 1277.3 reduce-scatter.1
  1299.9 119.8 all-gather.1
where the time goes:
time: 1430 us
  waiting for transfers between devices  1400 us (98%)
    reduce_scatter x1, waiting for transfers between devices, body(): lax.psum_scatter(code.astype(jnp.float32), ('dp', 'replica'), scatter_dim...  1280 us
    all_gather x1, waiting for transfers between devices, body(): weights = lax.all_gather(rounded, ('dp', 'replica'), axis=0, tiled=True)  123 us
  transfers between devices with their start and end apart: 2, of which 2 were waited for; matrix products, arithmetic and copies ran while one was open for 0% of the time, Pallas kernels for 0%

commit v1 on v0

v1 whole, which is shorter than its diff:
```python
import jax
import jax.numpy as jnp
from jax import lax
from jax.experimental import pallas as pl
from jax.experimental.pallas import tpu as pltpu
from jax.sharding import PartitionSpec as P

beta_first = 0.9
beta_second = 0.999
learn_rate = 0.2
decay_rate = 0.1
adam_eps = 1e-08
step_count = 100

MESH = pl.DeviceIdType.MESH
NX, NY, NZ = 4, 4, 8
TOK, D, COLS = 448, 8192, 256
CHUNK = D // NZ
ROWS = 32
HALF = COLS // 2


def kernel(a_hbm, g_hbm, master_hbm, first_hbm, second_hbm, state_ref, w_ref,
           g_ref, moments, abuf, code, sib, pair, got1, part1, got2, part2, got3,
           a_sem, in_sem, send_sem, sib_sem, rs1_sem, rs2_sem, rs3_sem, ag3_sem, ag2_sem, ag1_sem, agc_sem):
    dp, rep = lax.axis_index("dp"), lax.axis_index("replica")
    x, z, y, c = dp % NX, dp // NX, rep // 2, rep % 2
    bf16, f32 = jnp.bfloat16, jnp.float32

    def at(x, y, z, c):
        return (z * NX + x, y * 2 + c)

    def along_x(d):
        return (x + d) % NX

    def along_y(d):
        return (y + d) % NY

    def along_z(d):
        return (z + d) % NZ

    def z_shift(i):
        return jnp.where(i % 2 == 0, 4 + i // 2, (7 - i) // 2)

    def fetch(i):
        begin = pl.multiple_of(along_z(z_shift(i)) * CHUNK, CHUNK)
        return pltpu.make_async_copy(a_hbm.at[:, pl.ds(begin, CHUNK)], abuf.at[i], a_sem.at[i])

    def send(src, dst, stage, sem, target):
        return pltpu.make_async_remote_copy(
            src_ref=src, dst_ref=dst, send_sem=send_sem.at[stage], recv_sem=sem,
            device_id=target, device_id_type=MESH)

    def each(n, f, start=0):
        def step(i, carry):
            f(i)
            return carry
        lax.fori_loop(start, n, step, 0)

    def arrived(ref, sem):
        pltpu.make_async_remote_copy(
            src_ref=ref, dst_ref=ref, send_sem=send_sem.at[0], recv_sem=sem,
            device_id=at(x, y, z, 1 - c), device_id_type=MESH).wait_recv()

    def left(ref, stage):
        pltpu.make_async_remote_copy(
            src_ref=ref, dst_ref=ref, send_sem=send_sem.at[stage], recv_sem=sib_sem.at[0],
            device_id=at(x, y, z, 1 - c), device_id_type=MESH).wait_send()

    barrier = pltpu.get_barrier_semaphore()
    peers = [at(x, y, z, 1 - c)]
    peers += [at(along_x(d), y, z, c) for d in range(1, NX)]
    peers += [at(x, along_y(d), z, c) for d in range(1, NY)]
    peers += [at(x, y, along_z(d), c) for d in range(1, NZ)]
    for peer in peers:
        pl.semaphore_signal(barrier, inc=1, device_id=peer, device_id_type=MESH)
    loads = [pltpu.make_async_copy(g_hbm, g_ref, in_sem.at[0])]
    for i, ref in enumerate((master_hbm, first_hbm, second_hbm)):
        loads.append(pltpu.make_async_copy(ref, moments.at[i], in_sem.at[1 + i]))
    loads[0].start()
    each(NZ, lambda i: fetch(i).start())
    for load in loads[1:]:
        load.start()
    loads[0].wait()

    def multiply(i):
        fetch(i).wait()
        term = lax.dot_general(abuf[i], g_ref[...], (((0,), (0,)), ((), ())), preferred_element_type=f32)
        code[i] = term.astype(bf16).reshape(NX, NY, 2, ROWS, COLS)

    def send_sib(i):
        send(code.at[i, :, :, 1 - c], sib.at[i], 0, sib_sem.at[i], at(x, y, z, 1 - c)).start()

    def add_pair(i):
        arrived(sib.at[i], sib_sem.at[i])
        pair[i] = (code[i, :, :, c].astype(f32) + sib[i].astype(f32)).astype(bf16)

    def send_1(i):
        for d in (2, 1, 3):
            send(pair.at[i, along_x(d), :, :, pl.ds(0, HALF)], got1.at[i, d - 1], 1, rs1_sem.at[i],
                 at(along_x(d), y, z, c)).start()
            send(pair.at[i, :, along_y(d), :, pl.ds(HALF, HALF)], got1.at[i, 2 + d], 1, rs1_sem.at[i],
                 at(x, along_y(d), z, c)).start()

    def add_1(i):
        arrived(got1.at[i], rs1_sem.at[i])
        p = pair[i, x, :, :, 0:HALF].astype(f32)
        q = pair[i, :, y, :, HALF:COLS].astype(f32)
        for d in range(3):
            p = p + got1[i, d].astype(f32)
            q = q + got1[i, 3 + d].astype(f32)
        part1[i, 0] = p.astype(bf16)
        part1[i, 1] = q.astype(bf16)

    def send_2(i):
        for d in (2, 1, 3):
            send(part1.at[i, 0, along_y(d)], got2.at[i, d - 1], 2, rs2_sem.at[i], at(x, along_y(d), z, c)).start()
            send(part1.at[i, 1, along_x(d)], got2.at[i, 2 + d], 2, rs2_sem.at[i], at(along_x(d), y, z, c)).start()

    def add_2(i):
        arrived(got2.at[i], rs2_sem.at[i])
        p = part1[i, 0, y].astype(f32)
        q = part1[i, 1, x].astype(f32)
        for d in range(3):
            p = p + got2[i, d].astype(f32)
            q = q + got2[i, 3 + d].astype(f32)
        part2[i, :, 0:HALF] = p
        part2[i, :, HALF:COLS] = q

    def send_3(i):
        send(part2.at[i], got3.at[i], 3, rs3_sem.at[i], at(x, y, along_z(z_shift(i)), c)).start()

    multiply(0)
    pl.semaphore_wait(barrier, len(peers))
    send_sib(0)

    def phase_a(i):
        multiply(i)
        send_sib(i)

        @pl.when(i >= 2)
        def _():
            add_pair(i - 2)
            send_1(i - 2)
    each(NZ, phase_a, 1)

    def phase_a_end(i):
        add_pair(i)
        send_1(i)
    each(NZ, phase_a_end, NZ - 2)

    def phase_b(i):
        add_1(i)
        send_2(i)

        @pl.when(i >= 2)
        def _():
            add_2(i - 2)
            send_3(i - 2)
    each(NZ, phase_b)
    add_2(NZ - 2)
    send_3(NZ - 2)
    add_2(NZ - 1)

    for load in loads[1:]:
        load.wait()
    grad = part2[NZ - 1]
    for i in range(NZ - 1):
        arrived(got3.at[i], rs3_sem.at[i])
        grad = grad + got3[i]
    new_first = beta_first * moments[1] + (1.0 - beta_first) * grad
    new_second = beta_second * moments[2] + (1.0 - beta_second) * grad * grad
    first_hat = new_first / (1.0 - beta_first**step_count)
    second_hat = new_second / (1.0 - beta_second**step_count)
    master = moments[0]
    new_master = master - learn_rate * (
        first_hat / (jnp.sqrt(second_hat) + adam_eps) + decay_rate * master
    )
    w_ref[z, x, y, c] = new_master.astype(bf16)

    def gather_3(i):
        mine = w_ref.at[z, x, y, c]
        send(mine, mine, 4, ag3_sem.at[i], at(x, y, along_z(z_shift(i)), c)).start()
    each(NZ - 1, gather_3)
    state_ref[0] = grad
    state_ref[1] = new_master
    state_ref[2] = new_first
    state_ref[3] = new_second

    def z_of(j):
        return along_z(z_shift(NZ - 1 - j))

    def gather_2(j):
        @pl.when(j >= 1)
        def _():
            shift = (NZ - z_shift(NZ - 1 - j)) % NZ
            slot = jnp.where(shift >= 4, 2 * (shift - 4), 7 - 2 * shift)
            arrived(w_ref.at[0, 0, 0, 0], ag3_sem.at[slot])
        k = z_of(j)
        p = w_ref.at[k, x, y, c, :, pl.ds(0, HALF)]
        q = w_ref.at[k, x, y, c, :, pl.ds(HALF, HALF)]
        for d in (2, 1, 3):
            send(p, p, 5, ag2_sem.at[j], at(x, along_y(d), z, c)).start()
            send(q, q, 5, ag2_sem.at[j], at(along_x(d), y, z, c)).start()

    def gather_1(j):
        arrived(got2.at[0], ag2_sem.at[j])
        k = z_of(j)
        p = w_ref.at[k, x, :, c, :, pl.ds(0, HALF)]
        q = w_ref.at[k, :, y, c, :, pl.ds(HALF, HALF)]
        for d in (2, 1, 3):
            send(p, p, 6, ag1_sem.at[j], at(along_x(d), y, z, c)).start()
            send(q, q, 6, ag1_sem.at[j], at(x, along_y(d), z, c)).start()

    def gather_c(j):
        arrived(got1.at[0], ag1_sem.at[j])
        k = z_of(j)
        whole = w_ref.at[k, :, :, c]
        send(whole, whole, 7, agc_sem.at[j], at(x, y, z, 1 - c)).start()

    def phase_c(j):
        @pl.when(j < NZ)
        def _():
            gather_2(j)

        @pl.when((j >= 1) & (j < NZ + 1))
        def _():
            gather_1(j - 1)

        @pl.when(j >= 4)
        def _():
            gather_c(j - 4)
    each(NZ + 4, phase_c)

    each(NZ, lambda j: arrived(sib.at[0], agc_sem.at[j]))
    left(sib, 0)
    left(got1, 1)
    left(got2, 2)
    left(got3, 3)
    each(NZ - 1, lambda i: left(w_ref.at[0, 0, 0, 0], 4))
    left(got2, 5)
    left(got1, 6)
    left(sib, 7)


def finish(state_ref, w_ref, grad_ref, master_ref, first_ref, second_ref, out_ref, sem):
    copies = [pltpu.make_async_copy(w_ref, out_ref, sem.at[4])]
    for i, ref in enumerate((grad_ref, master_ref, first_ref, second_ref)):
        copies.append(pltpu.make_async_copy(state_ref.at[i], ref, sem.at[i]))
    for copy in copies:
        copy.start()
    for copy in copies:
        copy.wait()


def body(activations, out_grads, master, first_moment, second_moment):
    f32, bf16 = jnp.float32, jnp.bfloat16
    vmem = pl.BlockSpec(memory_space=pltpu.VMEM)
    anywhere = pl.BlockSpec(memory_space=pl.ANY)
    dma = pltpu.SemaphoreType.DMA
    state, w = pl.pallas_call(
        kernel,
        name="reduce_update_gather",
        out_shape=(
            pltpu.VMEM((4, ROWS, COLS), f32),
            pltpu.VMEM((NZ, NX, NY, 2, ROWS, COLS), bf16),
        ),
        in_specs=[anywhere] * 5,
        out_specs=(vmem, vmem),
        scratch_shapes=[
            pltpu.VMEM((TOK, COLS), bf16),
            pltpu.VMEM((3, ROWS, COLS), f32),
            pltpu.VMEM((NZ, TOK, CHUNK), bf16),
            pltpu.VMEM((NZ, NX, NY, 2, ROWS, COLS), bf16),
            pltpu.VMEM((NZ, NX, NY, ROWS, COLS), bf16),
            pltpu.VMEM((NZ, NX, NY, ROWS, COLS), bf16),
            pltpu.VMEM((NZ, 6, 4, ROWS, HALF), bf16),
            pltpu.VMEM((NZ, 2, 4, ROWS, HALF), bf16),
            pltpu.VMEM((NZ, 6, ROWS, HALF), bf16),
            pltpu.VMEM((NZ, ROWS, COLS), f32),
            pltpu.VMEM((NZ - 1, ROWS, COLS), f32),
            dma((NZ,)), dma((4,)), dma((8,)),
            dma((NZ,)), dma((NZ,)), dma((NZ,)), dma((NZ,)),
            dma((NZ,)), dma((NZ,)), dma((NZ,)), dma((NZ,)),
        ],
        compiler_params=pltpu.CompilerParams(
            collective_id=0, has_side_effects=True, vmem_limit_bytes=58 << 20
        ),
    )(activations, out_grads, master, first_moment, second_moment)
    row = jax.ShapeDtypeStruct((ROWS, COLS), f32)
    out = pl.pallas_call(
        finish,
        name="write_out",
        out_shape=(row, row, row, row, jax.ShapeDtypeStruct((NZ, NX, NY, 2, ROWS, COLS), bf16)),
        in_specs=[anywhere, anywhere],
        out_specs=(anywhere,) * 5,
        scratch_shapes=[dma((5,))],
        compiler_params=pltpu.CompilerParams(vmem_limit_bytes=1 << 20),
    )(state, w)
    return out[:4] + (out[4].reshape(D, COLS),)


def solution(mesh):
    spec = P(("dp", "replica"), None)
    return jax.shard_map(
        body, mesh=mesh, in_specs=(spec,) * 5, out_specs=(spec,) * 4 + (P(),), check_vma=False
    )
```

time: 1430 us -> 68.1 us (0.05)
  waiting for transfers between devices: 1400 us -> 0 us
  Pallas kernels: 0 us -> 67.4 us
    reduce_scatter x1 -> x0, waiting for transfers between devices: 1280 us -> none  [body(): lax.psum_scatter(code.astype(jnp.float32), ('dp', 'replica'), scatter_dim...]
    all_gather x1 -> x0, waiting for transfers between devices: 123 us -> none  [body(): weights = lax.all_gather(rounded, ('dp', 'replica'), axis=0, tiled=True)]
    pallas_call x0 -> x2, Pallas kernels: none -> 67.4 us  [the longest x1 65.3 us: body(): pl.pallas_call(kernel, name='reduce_update_gather', out_shape=(pltpu.VMEM...]
  transfers between devices with their start and end apart: 2 -> 0, of which waited for: 2 -> 0; matrix products, arithmetic and copies ran while one was open for 0% -> 0% of each run, Pallas kernels for 0% -> 0%
where the time goes in v1:
time: 68.1 us; the launch traced here: 68 us
  Pallas kernels  67.4 us (99%)
    pallas_call x1, Pallas kernels, body(): pl.pallas_call(kernel, name='reduce_update_gather', out_shape=(pltpu.VMEM...  65.3 us
    pallas_call x1, Pallas kernels, body(): pl.pallas_call(finish, name='write_out', out_shape=(row, row, row, row, j...  2.07 us

profile of v1, /device:TPU:1, one launch (start us, length us, event | category | flops | bytes accessed | tf_op | source)
XLA Modules:
  0.0 68.0 jit_solution(16818068938702309275)
XLA Ops:
  0.6 65.3 %reduce_update_gather.1 = (f32[4,32,256]{2,1,0:T(8,128)S(1)}, bf16[8,4,4,2,32,256]{5,4,3,2,1,0:T(8,128)(2,1)S(1)}) custom-call(bf16[448,8192]{1,0:T(8,128)(2,1)} %a_hbm.1, bf16[448,256]{1,0:T(8,128)(2,1)} %g_hbm.1, f32[32,256]{1,0:T(8,128)} %master_hbm.1, f32[32,256]{1,0:T(8,128)} %first_hbm.1, f32[32,256]{1,0:T(8,128)} %second_hbm.1), custom_call_target="tpu_custom_call" | custom-call | tf_op jit(solution)/shard_map/reduce_update_gather/pallas_call | solution.py:261
  66.0 2.1 %write_out.1 = (f32[32,256]{1,0:T(8,128)}, f32[32,256]{1,0:T(8,128)}, f32[32,256]{1,0:T(8,128)}, f32[32,256]{1,0:T(8,128)}, bf16[8,4,4,2,32,256]{5,4,3,2,1,0:T(8,128)(2,1)}) custom-call(f32[4,32,256]{2,1,0:T(8,128)S(1)} %get-tuple-element.12.state_ref, bf16[8,4,4,2,32,256]{5,4,3,2,1,0:T(8,128)(2,1)S(1)} %get-tuple-element.13.w_ref), custom_call_target="tpu_custom_call" | custom-call | tf_op jit(solution)/shard_map/write_out/pallas_call | solution.py:291

commit v2 on v1

--- a/solution.py
+++ b/solution.py
@@ -18,6 +18,8 @@
 CHUNK = D // NZ
 ROWS = 32
 HALF = COLS // 2
+AHEAD = 3
+LAGS = (2, 5, 8, 10, 13)
 
 
 def kernel(a_hbm, g_hbm, master_hbm, first_hbm, second_hbm, state_ref, w_ref,
@@ -39,11 +41,11 @@
     def along_z(d):
         return (z + d) % NZ
 
-    def z_shift(i):
-        return jnp.where(i % 2 == 0, 4 + i // 2, (7 - i) // 2)
+    def z_of(i):
+        return 4 * (i % 2) + 2 * (i // 2 % 2) + i // 4
 
     def fetch(i):
-        begin = pl.multiple_of(along_z(z_shift(i)) * CHUNK, CHUNK)
+        begin = pl.multiple_of(z_of(i) * CHUNK, CHUNK)
         return pltpu.make_async_copy(a_hbm.at[:, pl.ds(begin, CHUNK)], abuf.at[i], a_sem.at[i])
 
     def send(src, dst, stage, sem, target):
@@ -124,11 +126,64 @@
         for d in range(3):
             p = p + got2[i, d].astype(f32)
             q = q + got2[i, 3 + d].astype(f32)
-        part2[i, :, 0:HALF] = p
-        part2[i, :, HALF:COLS] = q
+        part2[i, :, 0:HALF] = p.astype(bf16)
+        part2[i, :, HALF:COLS] = q.astype(bf16)
 
     def send_3(i):
-        send(part2.at[i], got3.at[i], 3, rs3_sem.at[i], at(x, y, along_z(z_shift(i)), c)).start()
+        @pl.when(z != z_of(i))
+        def _():
+            slot = (z_of(i) - z + NZ - 1) % NZ
+            send(part2.at[i], got3.at[slot], 3, rs3_sem.at[0], at(x, y, z_of(i), c)).start()
+
+    def update(i):
+        for load in loads[1:]:
+            load.wait()
+        arrived(got3, rs3_sem.at[0])
+        grad = part2[i].astype(f32)
+        for d in range(NZ - 1):
+            grad = grad + got3[d].astype(f32)
+        new_first = beta_first * moments[1] + (1.0 - beta_first) * grad
+        new_second = beta_second * moments[2] + (1.0 - beta_second) * grad * grad
+        first_hat = new_first / (1.0 - beta_first**step_count)
+        second_hat = new_second / (1.0 - beta_second**step_count)
+        master = moments[0]
+        new_master = master - learn_rate * (
+            first_hat / (jnp.sqrt(second_hat) + adam_eps) + decay_rate * master
+        )
+        w_ref[z, x, y, c] = new_master.astype(bf16)
+        mine = w_ref.at[z, x, y, c]
+        for d in (4, 3, 5, 2, 6, 1, 7):
+            send(mine, mine, 4, ag3_sem.at[i], at(x, y, along_z(d), c)).start()
+        state_ref[0] = grad
+        state_ref[1] = new_master
+        state_ref[2] = new_first
+        state_ref[3] = new_second
+
+    def gather_2(i):
+        k = z_of(i)
+
+        @pl.when(z != k)
+        def _():
+            arrived(w_ref.at[0, 0, 0, 0], ag3_sem.at[i])
+        p = w_ref.at[k, x, y, c, :, pl.ds(0, HALF)]
+        q = w_ref.at[k, x, y, c, :, pl.ds(HALF, HALF)]
+        for d in (2, 1, 3):
+            send(p, p, 5, ag2_sem.at[i], at(x, along_y(d), z, c)).start()
+            send(q, q, 5, ag2_sem.at[i], at(along_x(d), y, z, c)).start()
+
+    def gather_1(i):
+        arrived(got2.at[0], ag2_sem.at[i])
+        k = z_of(i)
+        p = w_ref.at[k, x, :, c, :, pl.ds(0, HALF)]
+        q = w_ref.at[k, :, y, c, :, pl.ds(HALF, HALF)]
+        for d in (2, 1, 3):
+            send(p, p, 6, ag1_sem.at[i], at(along_x(d), y, z, c)).start()
+            send(q, q, 6, ag1_sem.at[i], at(x, along_y(d), z, c)).start()
+
+    def gather_c(i):
+        arrived(got1.at[0], ag1_sem.at[i])
+        whole = w_ref.at[z_of(i), :, :, c]
+        send(whole, whole, 7, agc_sem.at[i], at(x, y, z, 1 - c)).start()
 
     multiply(0)
     pl.semaphore_wait(barrier, len(peers))
@@ -141,96 +196,39 @@
         @pl.when(i >= 2)
         def _():
             add_pair(i - 2)
+
+        @pl.when((i >= 2) & (i < AHEAD + 2))
+        def _():
             send_1(i - 2)
     each(NZ, phase_a, 1)
 
     def phase_a_end(i):
         add_pair(i)
-        send_1(i)
+        pl.when(i < AHEAD)(lambda: send_1(i))
     each(NZ, phase_a_end, NZ - 2)
 
-    def phase_b(i):
-        add_1(i)
-        send_2(i)
-
-        @pl.when(i >= 2)
-        def _():
-            add_2(i - 2)
-            send_3(i - 2)
-    each(NZ, phase_b)
-    add_2(NZ - 2)
-    send_3(NZ - 2)
-    add_2(NZ - 1)
-
-    for load in loads[1:]:
-        load.wait()
-    grad = part2[NZ - 1]
-    for i in range(NZ - 1):
-        arrived(got3.at[i], rs3_sem.at[i])
-        grad = grad + got3[i]
-    new_first = beta_first * moments[1] + (1.0 - beta_first) * grad
-    new_second = beta_second * moments[2] + (1.0 - beta_second) * grad * grad
-    first_hat = new_first / (1.0 - beta_first**step_count)
-    second_hat = new_second / (1.0 - beta_second**step_count)
-    master = moments[0]
-    new_master = master - learn_rate * (
-        first_hat / (jnp.sqrt(second_hat) + adam_eps) + decay_rate * master
-    )
-    w_ref[z, x, y, c] = new_master.astype(bf16)
-
-    def gather_3(i):
-        mine = w_ref.at[z, x, y, c]
-        send(mine, mine, 4, ag3_sem.at[i], at(x, y, along_z(z_shift(i)), c)).start()
-    each(NZ - 1, gather_3)
-    state_ref[0] = grad
-    state_ref[1] = new_master
-    state_ref[2] = new_first
-    state_ref[3] = new_second
-
-    def z_of(j):
-        return along_z(z_shift(NZ - 1 - j))
-
-    def gather_2(j):
-        @pl.when(j >= 1)
-        def _():
-            shift = (NZ - z_shift(NZ - 1 - j)) % NZ
-            slot = jnp.where(shift >= 4, 2 * (shift - 4), 7 - 2 * shift)
-            arrived(w_ref.at[0, 0, 0, 0], ag3_sem.at[slot])
-        k = z_of(j)
-        p = w_ref.at[k, x, y, c, :, pl.ds(0, HALF)]
-        q = w_ref.at[k, x, y, c, :, pl.ds(HALF, HALF)]
-        for d in (2, 1, 3):
-            send(p, p, 5, ag2_sem.at[j], at(x, along_y(d), z, c)).start()
-            send(q, q, 5, ag2_sem.at[j], at(along_x(d), y, z, c)).start()
-
-    def gather_1(j):
-        arrived(got2.at[0], ag2_sem.at[j])
-        k = z_of(j)
-        p = w_ref.at[k, x, :, c, :, pl.ds(0, HALF)]
-        q = w_ref.at[k, :, y, c, :, pl.ds(HALF, HALF)]
-        for d in (2, 1, 3):
-            send(p, p, 6, ag1_sem.at[j], at(along_x(d), y, z, c)).start()
-            send(q, q, 6, ag1_sem.at[j], at(x, along_y(d), z, c)).start()
-
-    def gather_c(j):
-        arrived(got1.at[0], ag1_sem.at[j])
-        k = z_of(j)
-        whole = w_ref.at[k, :, :, c]
-        send(whole, whole, 7, agc_sem.at[j], at(x, y, z, 1 - c)).start()
-
-    def phase_c(j):
-        @pl.when(j < NZ)
-        def _():
-            gather_2(j)
-
-        @pl.when((j >= 1) & (j < NZ + 1))
-        def _():
-            gather_1(j - 1)
-
-        @pl.when(j >= 4)
-        def _():
-            gather_c(j - 4)
-    each(NZ + 4, phase_c)
+    def stage(s, lag, f):
+        pl.when((s >= lag) & (s < lag + NZ))(lambda: f(s - lag))
+
+    def phase_b(s):
+        def sum_1(i):
+            add_1(i)
+            send_2(i)
+            pl.when(i < NZ - AHEAD)(lambda: send_1(i + AHEAD))
+
+        def sum_2(i):
+            add_2(i)
+            send_3(i)
+
+        def own(i):
+            pl.when(z == z_of(i))(lambda: update(i))
+        stage(s, 0, sum_1)
+        stage(s, LAGS[0], sum_2)
+        stage(s, LAGS[1], own)
+        stage(s, LAGS[2], gather_2)
+        stage(s, LAGS[3], gather_1)
+        stage(s, LAGS[4], gather_c)
+    each(NZ + LAGS[4], phase_b)
 
     each(NZ, lambda j: arrived(sib.at[0], agc_sem.at[j]))
     left(sib, 0)
@@ -277,8 +275,8 @@
             pltpu.VMEM((NZ, 6, 4, ROWS, HALF), bf16),
             pltpu.VMEM((NZ, 2, 4, ROWS, HALF), bf16),
             pltpu.VMEM((NZ, 6, ROWS, HALF), bf16),
-            pltpu.VMEM((NZ, ROWS, COLS), f32),
-            pltpu.VMEM((NZ - 1, ROWS, COLS), f32),
+            pltpu.VMEM((NZ, ROWS, COLS), bf16),
+            pltpu.VMEM((NZ - 1, ROWS, COLS), bf16),
             dma((NZ,)), dma((4,)), dma((8,)),
             dma((NZ,)), dma((NZ,)), dma((NZ,)), dma((NZ,)),
             dma((NZ,)), dma((NZ,)), dma((NZ,)), dma((NZ,)),

time: 68.1 us -> 54.6 us (0.80)
  Pallas kernels: 67.4 us -> 53.9 us
    pallas_call x1, Pallas kernels: 65.3 us -> 51.8 us  [body(): pl.pallas_call(kernel, name='reduce_update_gather', out_shape=(pltpu.VMEM...]
where the time goes in v2:
time: 54.6 us; the launch traced here: 54.5 us
  Pallas kernels  53.9 us (99%)
  between operations  0.64 us (1%)
    pallas_call x1, Pallas kernels, body(): pl.pallas_call(kernel, name='reduce_update_gather', out_shape=(pltpu.VMEM...  51.8 us
    pallas_call x1, Pallas kernels, body(): pl.pallas_call(finish, name='write_out', out_shape=(row, row, row, row, j...  2.07 us

profile of v2, /device:TPU:1, one launch (start us, length us, event | category | flops | bytes accessed | tf_op | source)
XLA Modules:
  0.0 54.5 jit_solution(14448798084876370326)
XLA Ops:
  0.6 51.8 %reduce_update_gather.1 = (f32[4,32,256]{2,1,0:T(8,128)S(1)}, bf16[8,4,4,2,32,256]{5,4,3,2,1,0:T(8,128)(2,1)S(1)}) custom-call(bf16[448,8192]{1,0:T(8,128)(2,1)} %a_hbm.1, bf16[448,256]{1,0:T(8,128)(2,1)} %g_hbm.1, f32[32,256]{1,0:T(8,128)} %master_hbm.1, f32[32,256]{1,0:T(8,128)} %first_hbm.1, f32[32,256]{1,0:T(8,128)} %second_hbm.1), custom_call_target="tpu_custom_call" | custom-call | tf_op jit(solution)/shard_map/reduce_update_gather/pallas_call | solution.py:259
  52.5 2.1 %write_out.1 = (f32[32,256]{1,0:T(8,128)}, f32[32,256]{1,0:T(8,128)}, f32[32,256]{1,0:T(8,128)}, f32[32,256]{1,0:T(8,128)}, bf16[8,4,4,2,32,256]{5,4,3,2,1,0:T(8,128)(2,1)}) custom-call(f32[4,32,256]{2,1,0:T(8,128)S(1)} %get-tuple-element.12.state_ref, bf16[8,4,4,2,32,256]{5,4,3,2,1,0:T(8,128)(2,1)S(1)} %get-tuple-element.13.w_ref), custom_call_target="tpu_custom_call" | custom-call | tf_op jit(solution)/shard_map/write_out/pallas_call | solution.py:289

commit v3 on v2

--- a/solution.py
+++ b/solution.py
@@ -19,7 +19,7 @@
 ROWS = 32
 HALF = COLS // 2
 AHEAD = 3
-LAGS = (2, 5, 8, 10, 13)
+LAGS = (2, 5, 7, 9, 12)
 
 
 def kernel(a_hbm, g_hbm, master_hbm, first_hbm, second_hbm, state_ref, w_ref,
@@ -193,19 +193,19 @@
         multiply(i)
         send_sib(i)
 
-        @pl.when(i >= 2)
+        @pl.when(i >= 3)
         def _():
-            add_pair(i - 2)
-
-        @pl.when((i >= 2) & (i < AHEAD + 2))
+            add_pair(i - 3)
+
+        @pl.when((i >= 3) & (i < AHEAD + 3))
         def _():
-            send_1(i - 2)
+            send_1(i - 3)
     each(NZ, phase_a, 1)
 
     def phase_a_end(i):
         add_pair(i)
         pl.when(i < AHEAD)(lambda: send_1(i))
-    each(NZ, phase_a_end, NZ - 2)
+    each(NZ, phase_a_end, NZ - 3)
 
     def stage(s, lag, f):
         pl.when((s >= lag) & (s < lag + NZ))(lambda: f(s - lag))

time: 54.6 us -> 54.5 us (level)
  no operation moved by 1% of the time
where the time goes in v3:
time: 54.5 us; the launch traced here: 54.4 us
  Pallas kernels  53.7 us (99%)
  between operations  0.64 us (1%)
    pallas_call x1, Pallas kernels, body(): pl.pallas_call(kernel, name='reduce_update_gather', out_shape=(pltpu.VMEM...  51.7 us
    pallas_call x1, Pallas kernels, body(): pl.pallas_call(finish, name='write_out', out_shape=(row, row, row, row, j...  2.07 us

profile of v3, /device:TPU:1, one launch (start us, length us, event | category | flops | bytes accessed | tf_op | source)
XLA Modules:
  0.0 54.4 jit_solution(6319601671985269904)
XLA Ops:
  0.6 51.7 %reduce_update_gather.1 = (f32[4,32,256]{2,1,0:T(8,128)S(1)}, bf16[8,4,4,2,32,256]{5,4,3,2,1,0:T(8,128)(2,1)S(1)}) custom-call(bf16[448,8192]{1,0:T(8,128)(2,1)} %a_hbm.1, bf16[448,256]{1,0:T(8,128)(2,1)} %g_hbm.1, f32[32,256]{1,0:T(8,128)} %master_hbm.1, f32[32,256]{1,0:T(8,128)} %first_hbm.1, f32[32,256]{1,0:T(8,128)} %second_hbm.1), custom_call_target="tpu_custom_call" | custom-call | tf_op jit(solution)/shard_map/reduce_update_gather/pallas_call | solution.py:259
  52.3 2.1 %write_out.1 = (f32[32,256]{1,0:T(8,128)}, f32[32,256]{1,0:T(8,128)}, f32[32,256]{1,0:T(8,128)}, f32[32,256]{1,0:T(8,128)}, bf16[8,4,4,2,32,256]{5,4,3,2,1,0:T(8,128)(2,1)}) custom-call(f32[4,32,256]{2,1,0:T(8,128)S(1)} %get-tuple-element.12.state_ref, bf16[8,4,4,2,32,256]{5,4,3,2,1,0:T(8,128)(2,1)S(1)} %get-tuple-element.13.w_ref), custom_call_target="tpu_custom_call" | custom-call | tf_op jit(solution)/shard_map/write_out/pallas_call | solution.py:289
